TPU v7x, 32 devices: a whole 2x2x4 slice. The times are simulated.
32 devices in a mesh: parts: 1, row: 8 (over z, y), col: 1, depth: 4 (over x, core).
Axes of the slice: x: 2, y: 2, z: 4, core: 2. Of those that a mesh axis runs over, the one named last changes fastest.
Arguments:
- activations: bfloat16 [4, 256, 8192], P(('parts', 'depth'), 'row', 'col'), may hold values from -6 to 6
- hidden_grads: bfloat16 [4, 256, 16384], P(('parts', 'depth'), 'col', 'row'), may hold values from -0.1875 to 0.1875
Outputs:
- weight_grad: bfloat16 [8192, 16384], P(('parts', 'col', 'depth'), 'row')
All inputs are finite; a program needn't handle non-finite values.
Results may differ from a plain program's by a relative error of at most 0.013.
Values may be sent and summed in bfloat16 or wider, within the bound.
A program may use at most 128 MiB of HBM per device.

v0:
```python
import jax
import jax.numpy as jnp
from jax import lax
from jax.sharding import PartitionSpec as P


def local(activations, hidden_grads):
    swapped = lax.all_to_all(activations, "depth", split_axis=2, concat_axis=0, tiled=True)
    acts = lax.all_gather(swapped, "row", axis=1, tiled=True)
    grads = lax.all_gather(hidden_grads, "depth", axis=0, tiled=True)
    grads = lax.all_gather(grads, "col", axis=1, tiled=True)
    total = lax.dot_general(
        acts, grads, (((0, 1), (0, 1)), ((), ())), preferred_element_type=jnp.float32
    )
    return total.astype(jnp.bfloat16)


def solution(mesh):
    in_specs = (P(("parts", "depth"), "row", "col"), P(("parts", "depth"), "col", "row"))
    out_specs = P(("parts", "col", "depth"), "row")
    return jax.shard_map(local, mesh=mesh, in_specs=in_specs, out_specs=out_specs, check_vma=False)
```

profile of v0, /device:TPU:0, one launch (start us, length us, event | category | flops | bytes accessed | tf_op | source)
XLA Modules:
  0.0 217.2 jit_solution(3695399159835913625)
XLA Ops:
  6.5 0.0 all-gather.6.cloned.1.call-start
  6.5 8.6 %copy.7 = bf16[1,32,8192]{1,0,2:T(2,128)(2,1)} copy(bf16[1,32,8192]{2,1,0:T(8,128)(2,1)} %param.2) | data formatting | bytes 1048576 | tf_op args[0]
  15.1 0.5 broadcast
  15.6 45.2 %reduce = bf16[8192,32]{1,0:T(8,128)(2,1)S(1)} reduce(bf16[8192,1,32]{2,1,0:T(2,128)(2,1)} %bitcast.11, bf16[]{:T(256)} %broadcast), dimensions={1}, to_apply=%bitcast.8.reduce_sub_computation | reduce | bytes 1048578
  60.8 2.2 reshape.2
  63.0 12.9 %all_to_all.18 = bf16[4,2,32768]{2,1,0:T(2,128)(2,1)S(1)} all-to-all(bf16[4,2,32768]{2,1,0:T(2,128)(2,1)S(1)} %reshape.2), channel_id=1, replica_groups=mesh['parts'=1,'row'=8,'col'=1,'depth'=4] {'depth'}, dimensions={0} | all-to-all | bytes 1048576 | tf_op jit(solution)/shard_map/all_to_all | solution.py:8
  75.9 3.3 %reshape.3 = bf16[8192,1,32]{2,1,0:T(2,128)(2,1)} reshape(bf16[4,2,32768]{2,1,0:T(2,128)(2,1)S(1)} %all_to_all.18) | data formatting | bytes 1048576
  79.1 8.0 %copy.8 = bf16[1,32,8192]{2,1,0:T(8,128)(2,1)S(1)} copy(bf16[1,32,8192]{1,0,2:T(2,128)(2,1)} %bitcast.12) | data formatting | bytes 1048576 | tf_op jit(solution)/shard_map/all_to_all | solution.py:8
  87.1 1.2 all_to_all.14
  88.3 0.0 all-gather.6.cloned.1.call-update
  88.3 0.2 all-gather.4.cloned.1.call-start
  88.5 0.5 all-gather.4.cloned.1.call-update
  89.0 73.1 %all-gather.6.cloned.1.call-done = bf16[4,1,256,2048]{3,0,1,2:T(4,128)(2,1)} async-done(((bf16[4,1,32,2048]{3,0,1,2:T(4,128)(2,1)}), bf16[4,1,256,2048]{3,0,1,2:T(4,128)(2,1)}) %all-gather.6.cloned.1.call-update) | async-done | bytes 4194320 | tf_op jit(solution)/shard_map/all_gather | solution.py:9
  162.2 7.6 %copy.10 = bf16[4,1,256,2048]{2,3,0,1:T(8,128)(2,1)} copy(bf16[4,1,256,2048]{3,0,1,2:T(4,128)(2,1)} %all-gather.6.cloned.1.call-done) | data formatting | bytes 8388608 | tf_op jit(solution)/shard_map/all_gather | solution.py:9
  169.7 26.8 %all-gather.4.cloned.1.call-done = bf16[4,256,2048]{2,1,0:T(8,128)(2,1)} async-done(((bf16[1,256,2048]{2,1,0:T(8,128)(2,1)}), bf16[4,256,2048]{2,1,0:T(8,128)(2,1)}) %all-gather.4.cloned.1.call-update) | async-done | bytes 4194320 | tf_op jit(solution)/shard_map/all_gather | solution.py:10
  196.5 13.9 %bitcast_convert_fusion = bf16[2048,2048]{1,0:T(8,128)(2,1)} fusion(bf16[4,256,2048]{2,1,0:T(8,128)(2,1)} %all-gather.4.cloned.1.call-done, bf16[4,1,256,2048]{2,3,0,1:T(8,128)(2,1)} %copy.10), kind=kOutput, calls=%fused_computation | convolution fusion | flops 8594128896 | bytes 16777216 | tf_op jit(solution)/shard_map/dot_general | solution.py:12
Async XLA Ops:
  6.5 155.6 %all-gather.6.cloned.1.call-start = ((), (), s32[]{:S(2)}) async-start(), calls=%async_computation.2 | async-start | bytes 4718592 | tf_op jit(solution)/shard_map/all_gather | solution.py:9
  88.3 108.2 %all-gather.4.cloned.1.call-start = ((), (), s32[]{:S(2)}) async-start(), calls=%async_computation.1 | async-start | bytes 5242880 | tf_op jit(solution)/shard_map/all_gather | solution.py:10
Sparse Core Ops, SparseCore 0:
  88.4 73.7 all-gather.5
  163.7 32.7 all-gather.3
where the time goes:
time: 218 us; the launch traced here: 217 us
  waiting for transfers between devices  100 us (46%)
  other arithmetic  45.2 us (21%)
  local copies, waits for them, and re-layouts  31.2 us (14%)
  matrix products  13.9 us (6%)
  between operations  13.4 us (6%)
  blocking collectives  12.9 us (6%)
    all_gather x1, waiting for transfers between devices, local(): acts = lax.all_gather(swapped, 'row', axis=1, tiled=True)  73.1 us
    unnamed x1, other arithmetic  45.2 us
    all_gather x1, waiting for transfers between devices, local(): grads = lax.all_gather(hidden_grads, 'depth', axis=0, tiled=True)  26.8 us
    unnamed x4, local copies, waits for them, and re-layouts  14.5 us
    dot_general x1, matrix products, local(): lax.dot_general(acts, grads, (((0, 1), (0, 1)), ((), ())), preferred_elem...  13.9 us
    all_to_all x1, blocking collectives, local(): lax.all_to_all(activations, 'depth', split_axis=2, concat_axis=0, tiled=T...  12.9 us
    all_to_all x2, local copies, waits for them, and re-layouts, local(): lax.all_to_all(activations, 'depth', split_axis=2, concat_axis=0, tiled=T...  9.14 us
    all_gather x1, local copies, waits for them, and re-layouts, local(): acts = lax.all_gather(swapped, 'row', axis=1, tiled=True)  7.56 us
  transfers between devices with their start and end apart: 2, of which 2 were waited for; matrix products, arithmetic and copies ran while one was open for 3% of the time, Pallas kernels for 0%

commit v1 on v0

--- a/solution.py
+++ b/solution.py
@@ -5,7 +5,12 @@
 
 
 def local(activations, hidden_grads):
-    swapped = lax.all_to_all(activations, "depth", split_axis=2, concat_axis=0, tiled=True)
+    swapped = jnp.concatenate(
+        lax.all_to_all(
+            jnp.stack(jnp.split(activations, lax.axis_size("depth"), axis=2)), "depth", 0, 0
+        ),
+        axis=0,
+    )
     acts = lax.all_gather(swapped, "row", axis=1, tiled=True)
     grads = lax.all_gather(hidden_grads, "depth", axis=0, tiled=True)
     grads = lax.all_gather(grads, "col", axis=1, tiled=True)

time: 218 us -> 151 us (0.69)
  other arithmetic: 45.2 us -> 0.07 us
  local copies, waits for them, and re-layouts: 31.2 us -> 9.95 us
    unnamed x1 -> x0, other arithmetic: 45.2 us -> none
    unnamed x4 -> x0, local copies, waits for them, and re-layouts: 14.5 us -> none
    all_to_all x2 -> x1, local copies, waits for them, and re-layouts: 9.14 us -> 1.2 us  [local(): lax.all_to_all(jnp.stack(jnp.split(activations, lax.axis_size('depth'), a...]
  transfers between devices with their start and end apart: 2 -> 2, of which waited for: 2 -> 2; matrix products, arithmetic and copies ran while one was open for 3% -> 5% of each run, Pallas kernels for 0% -> 0%
where the time goes in v1:
time: 151 us
  waiting for transfers between devices  101 us (67%)
  matrix products  13.9 us (9%)
  between operations  13.4 us (9%)
  blocking collectives  12.9 us (9%)
  local copies, waits for them, and re-layouts  9.95 us (7%)
    all_gather x1, waiting for transfers between devices, local(): acts = lax.all_gather(swapped, 'row', axis=1, tiled=True)  73.1 us
    all_gather x1, waiting for transfers between devices, local(): grads = lax.all_gather(hidden_grads, 'depth', axis=0, tiled=True)  26.7 us
    dot_general x1, matrix products, local(): lax.dot_general(acts, grads, (((0, 1), (0, 1)), ((), ())), preferred_elem...  13.9 us
    all_to_all x1, blocking collectives, local(): lax.all_to_all(jnp.stack(jnp.split(activations, lax.axis_size('depth'), a...  12.9 us
    all_gather x1, local copies, waits for them, and re-layouts, local(): acts = lax.all_gather(swapped, 'row', axis=1, tiled=True)  7.62 us
  transfers between devices with their start and end apart: 2, of which 2 were waited for; matrix products, arithmetic and copies ran while one was open for 5% of the time, Pallas kernels for 0%

profile of v1, /device:TPU:0, one launch (start us, length us, event | category | flops | bytes accessed | tf_op | source)
XLA Modules:
  0.0 150.8 jit_solution(44746954799087093)
XLA Ops:
  6.5 0.0 all-gather.6.cloned.1.call-start
  6.5 1.1 slice_bitcast_fusion.3
  7.7 0.1 pad_maximum_fusion
  7.7 12.9 %all_to_all.5 = bf16[4,1,32,2048]{3,2,1,0:T(8,128)(2,1)S(1)} all-to-all(bf16[4,1,32,2048]{3,2,1,0:T(8,128)(2,1)S(1)} %pad_maximum_fusion), channel_id=1, replica_groups=mesh['parts'=1,'row'=8,'col'=1,'depth'=4] {'depth'}, dimensions={0} | all-to-all | bytes 1048576 | tf_op jit(solution)/shard_map/all_to_all | solution.py:9
  20.6 1.2 copy.7
  21.8 0.0 all-gather.6.cloned.1.call-update
  21.8 0.0 all-gather.4.cloned.1.call-start
  21.9 0.7 all-gather.4.cloned.1.call-update
  22.6 73.1 %all-gather.6.cloned.1.call-done = bf16[4,1,256,2048]{3,0,1,2:T(4,128)(2,1)} async-done(((bf16[4,1,32,2048]{3,0,1,2:T(4,128)(2,1)}), bf16[4,1,256,2048]{3,0,1,2:T(4,128)(2,1)}) %all-gather.6.cloned.1.call-update) | async-done | bytes 4194320 | tf_op jit(solution)/shard_map/all_gather | solution.py:14
  95.7 7.6 %copy.8 = bf16[4,1,256,2048]{2,3,0,1:T(8,128)(2,1)} copy(bf16[4,1,256,2048]{3,0,1,2:T(4,128)(2,1)} %all-gather.6.cloned.1.call-done) | data formatting | bytes 8388608 | tf_op jit(solution)/shard_map/all_gather | solution.py:14
  103.3 26.7 %all-gather.4.cloned.1.call-done = bf16[4,256,2048]{2,1,0:T(8,128)(2,1)} async-done(((bf16[1,256,2048]{2,1,0:T(8,128)(2,1)}), bf16[4,256,2048]{2,1,0:T(8,128)(2,1)}) %all-gather.4.cloned.1.call-update) | async-done | bytes 4194320 | tf_op jit(solution)/shard_map/all_gather | solution.py:15
  130.0 13.9 %bitcast_convert_fusion = bf16[2048,2048]{1,0:T(8,128)(2,1)} fusion(bf16[4,256,2048]{2,1,0:T(8,128)(2,1)} %all-gather.4.cloned.1.call-done, bf16[4,1,256,2048]{2,3,0,1:T(8,128)(2,1)} %copy.8), kind=kOutput, calls=%fused_computation | convolution fusion | flops 8594128896 | bytes 16777216 | tf_op jit(solution)/shard_map/dot_general | solution.py:17
Async XLA Ops:
  6.5 89.2 %all-gather.6.cloned.1.call-start = ((), (), s32[]{:S(2)}) async-start(), calls=%async_computation.2 | async-start | bytes 4718592 | tf_op jit(solution)/shard_map/all_gather | solution.py:14
  21.8 108.2 %all-gather.4.cloned.1.call-start = ((), (), s32[]{:S(2)}) async-start(), calls=%async_computation.1 | async-start | bytes 5242880 | tf_op jit(solution)/shard_map/all_gather | solution.py:15
Sparse Core Ops, SparseCore 0:
  21.9 73.7 all-gather.5
  97.3 32.7 all-gather.3
